TPU v7x, 32 devices: a whole 2x2x4 slice. The times are simulated.
32 devices in a mesh: group: 2 (over x), narrow: 16 (over z, y, core).
Axes of the slice: x: 2, y: 2, z: 4, core: 2. Of those that a mesh axis runs over, the one named last changes fastest.
Arguments:
- prefill_rows: bfloat16 [32, 6144], P(('group', 'narrow')), parts along dimension 0, may hold values from -6 to 6
- decode_rows: bfloat16 [32, 3, 6144], P(('group', 'narrow')), parts along dimension 0, may hold values from -6 to 6
- kv_cache: bfloat16 [32, 2048, 256], P(('group', 'narrow')), parts along dimension 0, may hold values from -300 to 300, as said below
- slot_lengths: int32 [32], P(('group', 'narrow')), parts along dimension 0, may hold values from 1 to 2048
- prefill_slot: int32 [2], P('group'), parts along dimension 0, may hold values from 0 to 15
- norm_gain: float32 [6144], replicated, may hold values from 0.1 to 1.9
- query_weight: bfloat16 [6144, 6144], P(None, 'narrow'), may hold values from -0.1875 to 0.1875
- keyval_weight: bfloat16 [6144, 256], P('narrow'), may hold values from -0.078125 to 0.078125
- output_weight: bfloat16 [6144, 6144], P('narrow'), may hold values from -0.21875 to 0.21875
Outputs:
- prefill_out: bfloat16 [32, 6144], P(('group', 'narrow')), parts along dimension 0
- decode_out: bfloat16 [32, 3, 6144], P(('group', 'narrow')), parts along dimension 0
There are 2 independent parts, one for each index of `group`. A program takes and returns all parts, laid end to end along the dimension named above; an argument that names none is the same for every part. Nothing has to cross between parts.
Inputs may be any that keep to these rules, and one draw needn't show every extreme that they name: `kv_cache`: entries are of order one in the values; key entries may be far larger.
All inputs are finite; a program needn't handle non-finite values.
Results may differ from a plain program's by a relative error of at most 0.0075.
The roundings to bfloat16 on the way count: a program that leaves them out, or rounds other values in their place, can miss the bound.
Values may be sent and summed in bfloat16 or wider, within the bound.
A program may use at most 64 MiB of HBM per device.

v0:
```python
import jax
import jax.numpy as jnp
from jax import lax
from jax.sharding import PartitionSpec as P

HEADS = 48
HEAD_DIM = 128
CACHE = 2048
PRE_DEV = 1
STEPS = 3


EPSILON = 1e-05


def layer_norm(inputs, gain):
    values = inputs.astype(jnp.float32)
    center = values - jnp.mean(values, axis=-1, keepdims=True)
    spread = jnp.mean(center * center, axis=-1, keepdims=True)
    return (center * lax.rsqrt(spread + EPSILON) * gain).astype(jnp.bfloat16)


def merge_block(state, queries, keyvals, allowed):
    highest, total, accum = state
    scores = jnp.einsum(
        "srhd,skd->srhk", queries, keyvals[..., :HEAD_DIM], preferred_element_type=jnp.float32
    )
    scores = scores * HEAD_DIM ** (-0.5)
    masked = jnp.where(allowed, scores, -1e30)
    new_high = jnp.maximum(highest, jnp.max(masked, axis=-1))
    weights = jnp.where(allowed, jnp.exp(scores - new_high[..., None]), 0.0)
    factor = jnp.exp(highest - new_high)
    total = total * factor + jnp.sum(weights, axis=-1)
    update = jnp.einsum(
        "srhk,skd->srhd",
        weights.astype(jnp.bfloat16),
        keyvals[..., HEAD_DIM:],
        preferred_element_type=jnp.float32,
    )
    accum = accum * factor[..., None] + update
    return (new_high, total, accum)


def per_device(
    prefill_rows,
    decode_rows,
    kv_cache,
    slot_lengths,
    prefill_slot,
    norm_gain,
    query_weight,
    keyval_weight,
    output_weight,
):
    devices = lax.axis_size("narrow")
    rank = lax.axis_index("narrow")
    prefill_total = PRE_DEV * devices
    row_width = keyval_weight.shape[0]
    row_start = rank * row_width
    width = HEADS * HEAD_DIM
    slot_count = kv_cache.shape[0]
    gathered = lax.all_gather(prefill_rows, "narrow", axis=0, tiled=True)
    normed = layer_norm(gathered, norm_gain)
    query_local = jnp.dot(normed, query_weight, preferred_element_type=jnp.float32).astype(
        jnp.bfloat16
    )
    normed_part = lax.dynamic_slice_in_dim(normed, row_start, row_width, 1)
    partial_kv = jnp.dot(normed_part, keyval_weight, preferred_element_type=jnp.float32)
    keyvals = lax.psum(partial_kv, "narrow").astype(jnp.bfloat16)
    own_queries = lax.all_to_all(query_local, "narrow", split_axis=0, concat_axis=1, tiled=True)
    own_queries = own_queries.reshape(1, PRE_DEV, HEADS, HEAD_DIM)
    own_pos = rank * PRE_DEV + jnp.arange(PRE_DEV, dtype=jnp.int32)
    key_pos = jnp.arange(prefill_total, dtype=jnp.int32)
    allowed = (key_pos[None, :] <= own_pos[:, None])[None, :, None, :]
    start_state = (
        jnp.full((1, PRE_DEV, HEADS), -1e30, jnp.float32),
        jnp.zeros((1, PRE_DEV, HEADS), jnp.float32),
        jnp.zeros((1, PRE_DEV, HEADS, HEAD_DIM), jnp.float32),
    )
    highest, total, accum = merge_block(start_state, own_queries, keyvals[None], allowed)
    pre_mixed = (accum / total[..., None]).astype(jnp.bfloat16).reshape(PRE_DEV, width)
    pre_back = lax.all_to_all(pre_mixed, "narrow", split_axis=1, concat_axis=0, tiled=True)
    rows = pre_back
    prefill_out = lax.psum_scatter(
        jnp.dot(rows, output_weight, preferred_element_type=jnp.float32),
        "narrow",
        scatter_dimension=0,
        tiled=True,
    ).astype(jnp.bfloat16)
    slot_ids = rank * slot_count + jnp.arange(slot_count, dtype=jnp.int32)
    chosen = slot_ids == prefill_slot[0]
    live_length = jnp.where(chosen, prefill_total, slot_lengths)
    block = min(512, CACHE)
    padded_prefill = jnp.concatenate(
        [keyvals, jnp.zeros((block - prefill_total, 2 * HEAD_DIM), jnp.bfloat16)], axis=0
    )
    block_count = CACHE // block
    gathered = lax.all_gather(decode_rows, "narrow", axis=0, tiled=True)
    normed = layer_norm(gathered, norm_gain)
    query_local = jnp.einsum(
        "ste,ec->stc", normed, query_weight, preferred_element_type=jnp.float32
    ).astype(jnp.bfloat16)
    normed_part = lax.dynamic_slice_in_dim(normed, row_start, row_width, 2)
    partial_kv = jnp.einsum(
        "ste,ec->stc", normed_part, keyval_weight, preferred_element_type=jnp.float32
    )
    fresh = lax.psum_scatter(partial_kv, "narrow", scatter_dimension=0, tiled=True).astype(
        jnp.bfloat16
    )
    own_queries = lax.all_to_all(query_local, "narrow", split_axis=0, concat_axis=2, tiled=True)
    own_queries = own_queries.reshape(slot_count, STEPS, HEADS, HEAD_DIM)
    queries = own_queries
    query_rows = queries.shape[1]
    state = (
        jnp.full((slot_count, query_rows, HEADS), -1e30, jnp.float32),
        jnp.zeros((slot_count, query_rows, HEADS), jnp.float32),
        jnp.zeros((slot_count, query_rows, HEADS, HEAD_DIM), jnp.float32),
    )

    def visit(block_index, carry):
        start = block_index * block
        rows = lax.dynamic_slice_in_dim(kv_cache, start, block, 1)
        position = start + jnp.arange(block, dtype=jnp.int32)
        replace = jnp.logical_and(chosen[:, None, None], (position < prefill_total)[None, :, None])
        rows = jnp.where(replace, padded_prefill[None], rows)
        valid = position[None, :] < live_length[:, None]
        return merge_block(carry, queries, rows, valid[:, None, None, :])

    state = lax.fori_loop(0, block_count, visit, state)
    fresh_valid = (
        jnp.arange(STEPS, dtype=jnp.int32)[None, :] <= jnp.arange(STEPS, dtype=jnp.int32)[:, None]
    )
    highest, total, accum = merge_block(state, queries, fresh, fresh_valid[None, :, None, :])
    mixed = (accum / total[..., None]).astype(jnp.bfloat16).reshape(slot_count, STEPS, width)
    back = lax.all_to_all(mixed, "narrow", split_axis=2, concat_axis=0, tiled=True)
    rows = back
    decode_out = lax.psum_scatter(
        jnp.einsum("stc,ce->ste", rows, output_weight, preferred_element_type=jnp.float32),
        "narrow",
        scatter_dimension=0,
        tiled=True,
    ).astype(jnp.bfloat16)
    return (prefill_out, decode_out)


def solution(mesh):
    in_specs = (
        P(("group", "narrow"), None),
        P(("group", "narrow"), None, None),
        P(("group", "narrow"), None, None),
        P(("group", "narrow")),
        P("group"),
        P(),
        P(None, "narrow"),
        P("narrow", None),
        P("narrow", None),
    )
    out_specs = (P(("group", "narrow"), None), P(("group", "narrow"), None, None))
    return jax.shard_map(
        per_device, mesh=mesh, in_specs=in_specs, out_specs=out_specs, check_vma=False
    )
```

profile of v0, /device:TPU:0, one launch (start us, length us, event | category | flops | bytes accessed | tf_op | source)
XLA Modules:
  0.0 291.9 jit_solution(6941363734331564194)
XLA Ops:
  0.6 24.5 %all-gather = bf16[16,1,6144]{2,1,0:T(2,128)(2,1)S(1)} all-gather(bf16[1,1,6144]{2,1,0:T(2,128)(2,1)} %bitcast.168), channel_id=1, replica_groups=mesh['group'=2,'narrow'=16] {'narrow'}, dimensions={0}, use_global_device_ids=true | all-gather | bytes 208896 | tf_op jit(solution)/shard_map/all_gather | solution.py:62
  26.4 0.9 multiply_convert_fusion
  27.3 3.1 %fusion.27 = bf16[16,1,384]{2,0,1:T(8,128)(2,1)S(1)} fusion(bf16[16,6144]{1,0:T(8,128)(2,1)S(1)} %multiply_convert_fusion, bf16[6144,384]{1,0:T(8,128)(2,1)} %param.17), kind=kOutput, calls=%fused_computation.45 | convolution fusion | flops 75503616 | bytes 4927488 | tf_op jit(solution)/shard_map/dot_general | solution.py:64
  31.6 0.7 reshape.274
  32.3 3.5 %all-to-all-start = ((bf16[16,2,192]{2,1,0:T(2,128)(2,1)}), bf16[16,2,192]{2,1,0:T(2,128)(2,1)S(1)}, u32[]{:S(2)}, u32[]{:S(2)}) async-start(bf16[16,2,192]{2,1,0:T(2,128)(2,1)} %reshape.274), calls=%async_computation | async-start | bytes 32768 | tf_op jit(solution)/shard_map/all_to_all | solution.py:70
  35.8 24.0 %all_gather.7 = bf16[16,3,6144]{2,1,0:T(4,128)(2,1)S(1)} all-gather(bf16[1,3,6144]{2,1,0:T(4,128)(2,1)S(1)} %copy-done.3), channel_id=1, replica_groups=mesh['group'=2,'narrow'=16] {'narrow'}, dimensions={0}, use_global_device_ids=true | all-gather | bytes 626688 | tf_op jit(solution)/shard_map/all_gather | solution.py:98
  59.8 0.7 convert_reduce_fusion
  60.6 0.7 fusion.16
  62.1 3.1 %fusion.22 = bf16[16,3,384]{2,0,1:T(8,128)(2,1)S(1)} fusion(bf16[16,3,6144]{2,0,1:T(8,128)(2,1)S(1)} %fusion.18, bf16[6144,384]{1,0:T(8,128)(2,1)} %param.17), kind=kOutput, calls=%fused_computation.40 | convolution fusion | flops 226510848 | bytes 5345280 | tf_op jit(solution)/shard_map/ste,ec->stc/dot_general | solution.py:100
  65.2 57.9 %all-reduce.5 = (bf16[16,256]{1,0:T(8,128)(2,1)S(1)}, bf16[16,3,256]{2,0,1:T(8,128)(2,1)S(1)}) all-reduce(f32[16,256]{1,0:T(8,128)S(1)} %fusion.35, f32[16,3,256]{2,0,1:T(8,128)S(1)} %fusion.28), channel_id=1, replica_groups=mesh['group'=2,'narrow'=16] {'narrow'}, use_global_device_ids=true, to_apply=%region_2.0 | all-reduce | flops 16384 | bytes 98304 | tf_op jit(solution)/shard_map/psum | solution.py:69
  125.2 0.7 reduce.20
  125.9 0.7 reshape.276
  126.6 3.5 %all-to-all-start.1 = ((bf16[16,2,192]{2,1,0:T(2,128)(2,1)}), bf16[16,2,192]{2,1,0:T(2,128)(2,1)S(1)}, u32[]{:S(2)}, u32[]{:S(2)}) async-start(bf16[16,2,192]{2,1,0:T(2,128)(2,1)} %reshape.276), calls=%async_computation.1 | async-start | bytes 32768 | tf_op jit(solution)/shard_map/all_to_all | solution.py:82
  132.1 4.4 %all-to-all-done.1 = bf16[16,2,192]{2,1,0:T(2,128)(2,1)S(1)} async-done(((bf16[16,2,192]{2,1,0:T(2,128)(2,1)}), bf16[16,2,192]{2,1,0:T(2,128)(2,1)S(1)}, u32[]{:S(2)}, u32[]{:S(2)}) %all-to-all-start.1) | async-done | bytes 12320 | tf_op jit(solution)/shard_map/all_to_all | solution.py:82
  136.5 3.7 %all-to-all-start.2 = ((bf16[16,3,384]{2,1,0:T(4,128)(2,1)}), bf16[16,3,384]{2,1,0:T(4,128)(2,1)S(1)}, u32[]{:S(2)}, u32[]{:S(2)}) async-start(bf16[16,3,384]{2,1,0:T(4,128)(2,1)} %copy.26), calls=%async_computation.2 | async-start | bytes 98304 | tf_op jit(solution)/shard_map/all_to_all | solution.py:110
  140.3 6.4 %all-to-all-done.2 = bf16[16,3,384]{2,1,0:T(4,128)(2,1)S(1)} async-done(((bf16[16,3,384]{2,1,0:T(4,128)(2,1)}), bf16[16,3,384]{2,1,0:T(4,128)(2,1)S(1)}, u32[]{:S(2)}, u32[]{:S(2)}) %all-to-all-start.2) | async-done | bytes 36896 | tf_op jit(solution)/shard_map/all_to_all | solution.py:110
  146.8 7.7 %while.18 = (s32[]{:T(128)}, f32[1,3,48]{2,1,0:T(4,128)S(1)}, f32[1,3,48]{2,1,0:T(4,128)S(1)}, f32[1,3,48,128]{3,2,1,0:T(8,128)S(1)}, s32[1]{0:T(128)}, /*index=...) while((s32[]{:T(128)}, f32[1,3,48]{2,1,0:T(4,128)S(1)}, ...), condition=%wide.region_11.12_spmd.clone, body=%wide.region_8.0_spmd.clone.sunk | while | flops 38601576 | bytes 2133060 | solution.py:129
  146.9 1.1 bitcast_select_fusion.2
  148.8 1.1 bitcast_select_fusion.2
  150.7 1.1 bitcast_select_fusion.2
  152.7 1.1 bitcast_select_fusion.2
  155.2 4.1 %copy.29 = bf16[1,3,6144]{1,0,2:T(2,128)(2,1)S(1)} copy(bf16[1,3,6144]{2,1,0:T(4,128)(2,1)S(1)} %reshape.250) | data formatting | bytes 73728 | tf_op jit(solution)/shard_map/reshape | solution.py:134
  159.3 34.4 %reduce.21 = bf16[6144,3]{1,0:T(8,128)(2,1)} reduce(bf16[6144,1,3]{2,1,0:T(2,128)(2,1)S(1)} %bitcast.160, bf16[]{:T(256)} %broadcast.236), dimensions={1}, to_apply=%bitcast.118.reduce_sub_computation | reduce | bytes 73730
  193.7 3.9 %reshape.278 = bf16[16,2,576]{2,1,0:T(2,128)(2,1)} reshape(bf16[6144,3]{1,0:T(8,128)(2,1)} %reduce.21) | data formatting | bytes 73728
  197.6 3.5 %all-to-all-start.3 = ((bf16[16,2,576]{2,1,0:T(2,128)(2,1)}), bf16[16,2,576]{2,1,0:T(2,128)(2,1)S(1)}, u32[]{:S(2)}, u32[]{:S(2)}) async-start(bf16[16,2,576]{2,1,0:T(2,128)(2,1)} %reshape.278), calls=%async_computation.3 | async-start | bytes 81920 | tf_op jit(solution)/shard_map/all_to_all | solution.py:135
  201.1 3.8 %fusion.32 = f32[16,6144]{1,0:T(8,128)} fusion(bf16[384,6144]{1,0:T(8,128)(2,1)} %param.19, bf16[1,16,384]{2,0,1:T(2,128)(2,1)S(1)} %bitcast.167), kind=kOutput, calls=%fused_computation.58 | convolution fusion | flops 75497472 | bytes 5124096 | tf_op jit(solution)/shard_map/dot_general | solution.py:85
  204.9 2.9 all-to-all-done.3
  207.8 3.3 %reshape.279 = bf16[6144,1,3]{2,1,0:T(2,128)(2,1)S(1)} reshape(bf16[16,2,576]{2,1,0:T(2,128)(2,1)S(1)} %all-to-all-done.3) | data formatting | bytes 73728
  211.1 2.9 %copy.30 = bf16[1,3,6144]{2,1,0:T(4,128)(2,1)S(1)} copy(bf16[1,3,6144]{1,0,2:T(2,128)(2,1)S(1)} %bitcast.161) | data formatting | bytes 73728 | tf_op jit(solution)/shard_map/all_to_all | solution.py:135
  214.1 3.3 %fusion.10 = f32[16,3,6144]{2,0,1:T(8,128)S(1)} fusion(bf16[384,6144]{1,0:T(8,128)(2,1)} %param.19, bf16[1,3,16,384]{3,1,2,0:T(4,128)(2,1)S(1)} %bitcast.165), kind=kOutput, calls=%fused_computation.25 | convolution fusion | flops 226492416 | bytes 5935104 | tf_op jit(solution)/shard_map/stc,ce->ste/dot_general | solution.py:138
  217.4 71.9 %all-reduce.7 = (bf16[16,6144]{1,0:T(8,128)(2,1)S(1)}, bf16[16,3,6144]{2,0,1:T(8,128)(2,1)S(1)}) all-reduce(f32[16,6144]{1,0:T(8,128)S(1)} %copy-done.1, f32[16,3,6144]{2,0,1:T(8,128)S(1)} %fusion.10), channel_id=2, replica_groups=mesh['group'=2,'narrow'=16] {'narrow'}, use_global_device_ids=true, to_apply=%region_5.6.clone | all-reduce | flops 393216 | bytes 2359296
  290.6 1.2 dynamic-slice_convert_fusion.1
  (82 shorter events, 11.1 us)
Async XLA Ops:
  0.6 61.1 %copy-start = (bf16[384,256]{1,0:T(8,128)(2,1)S(1)}, bf16[384,256]{1,0:T(8,128)(2,1)}, u32[]{:S(2)}) copy-start(bf16[384,256]{1,0:T(8,128)(2,1)} %param.18) | copy-start | bytes 589828
  25.6 10.2 %copy-start.3 = (bf16[1,3,6144]{2,1,0:T(4,128)(2,1)S(1)}, bf16[1,3,6144]{2,1,0:T(4,128)(2,1)}, u32[]{:S(2)}) copy-start(bf16[1,3,6144]{2,1,0:T(4,128)(2,1)} %param.12) | copy-start | bytes 110596
  27.3 34.0 %copy-start.2 = (f32[6144]{0:T(1024)S(1)}, f32[6144]{0:T(1024)}, u32[]{:S(2)}) copy-start(f32[6144]{0:T(1024)} %param.16) | copy-start | bytes 73732
  32.3 92.1 %all-to-all-start = ((bf16[16,2,192]{2,1,0:T(2,128)(2,1)}), bf16[16,2,192]{2,1,0:T(2,128)(2,1)S(1)}, u32[]{:S(2)}, u32[]{:S(2)}) async-start(bf16[16,2,192]{2,1,0:T(2,128)(2,1)} %reshape.274), calls=%async_computation | async-start | bytes 32768 | tf_op jit(solution)/shard_map/all_to_all | solution.py:70
  62.1 61.1 %copy-start.4 = (u32[32]{0:T(128)S(1)}, u32[32]{0:T(128)}, u32[]{:S(2)}) copy-start(u32[32]{0:T(128)} %constant.107) | copy-start | bytes 388
  126.6 10.0 %all-to-all-start.1 = ((bf16[16,2,192]{2,1,0:T(2,128)(2,1)}), bf16[16,2,192]{2,1,0:T(2,128)(2,1)S(1)}, u32[]{:S(2)}, u32[]{:S(2)}) async-start(bf16[16,2,192]{2,1,0:T(2,128)(2,1)} %reshape.276), calls=%async_computation.1 | async-start | bytes 32768 | tf_op jit(solution)/shard_map/all_to_all | solution.py:82
  136.5 10.2 %all-to-all-start.2 = ((bf16[16,3,384]{2,1,0:T(4,128)(2,1)}), bf16[16,3,384]{2,1,0:T(4,128)(2,1)S(1)}, u32[]{:S(2)}, u32[]{:S(2)}) async-start(bf16[16,3,384]{2,1,0:T(4,128)(2,1)} %copy.26), calls=%async_computation.2 | async-start | bytes 98304 | tf_op jit(solution)/shard_map/all_to_all | solution.py:110
  197.6 10.2 %all-to-all-start.3 = ((bf16[16,2,576]{2,1,0:T(2,128)(2,1)}), bf16[16,2,576]{2,1,0:T(2,128)(2,1)S(1)}, u32[]{:S(2)}, u32[]{:S(2)}) async-start(bf16[16,2,576]{2,1,0:T(2,128)(2,1)} %reshape.278), calls=%async_computation.3 | async-start | bytes 81920 | tf_op jit(solution)/shard_map/all_to_all | solution.py:135
  214.1 3.4 %copy-start.1 = (f32[16,6144]{1,0:T(8,128)S(1)}, f32[16,6144]{1,0:T(8,128)}, u32[]{:S(2)}) copy-start(f32[16,6144]{1,0:T(8,128)} %fusion.32) | copy-start | bytes 1179652
where the time goes:
time: 293 us; the launch traced here: 292 us
  blocking collectives  178 us (61%)
  other arithmetic  45.4 us (15%)
  local copies, waits for them, and re-layouts  21.1 us (7%)
  matrix products  16.7 us (6%)
  starting transfers between devices  14.2 us (5%)
  waiting for transfers between devices  13.7 us (5%)
    unnamed x1, blocking collectives  71.9 us
    psum x1, blocking collectives, per_device(): keyvals = lax.psum(partial_kv, 'narrow').astype(jnp.bfloat16)  57.9 us
    unnamed x5, other arithmetic  35.2 us
    all_gather x1, blocking collectives, per_device(): gathered = lax.all_gather(prefill_rows, 'narrow', axis=0, tiled=True)  24.5 us
    all_gather x1, blocking collectives, per_device(): gathered = lax.all_gather(decode_rows, 'narrow', axis=0, tiled=True)  24 us
    unnamed x18, local copies, waits for them, and re-layouts  10.1 us
    all_to_all x1, waiting for transfers between devices, per_device(): lax.all_to_all(query_local, 'narrow', split_axis=0, concat_axis=2, tiled=...  6.44 us
  transfers between devices with their start and end apart: 4, of which 3 were waited for; matrix products, arithmetic and copies ran while one was open for 4% of the time, Pallas kernels for 0%

commit v1 on v0

v1 whole, which is shorter than its diff:
```python
import functools

import jax
import jax.numpy as jnp
from jax import lax
from jax.experimental import pallas as pl
from jax.experimental.pallas import tpu as pltpu
from jax.sharding import PartitionSpec as P

HEAD_DIM = 128
EPSILON = 1e-05
MESH = pl.DeviceIdType.MESH
VMEM = pl.BlockSpec(memory_space=pltpu.VMEM)
SMEM = pl.BlockSpec(memory_space=pltpu.SMEM)
LIMIT = 40 * 1024 * 1024


def greet(n, me):
    barrier = pltpu.get_barrier_semaphore()

    def hello(k, carry):
        peer = lax.rem(me + k, n)
        pl.semaphore_signal(barrier, inc=1, device_id={"narrow": peer}, device_id_type=MESH)
        return carry

    lax.fori_loop(1, n, hello, 0)
    return barrier


def remote(src, dst, send, recv, peer):
    return pltpu.make_async_remote_copy(
        src_ref=src,
        dst_ref=dst,
        send_sem=send,
        recv_sem=recv,
        device_id={"narrow": peer},
        device_id_type=MESH,
    )


def each(start, stop, body):
    def step(k, carry):
        body(k)
        return carry

    lax.fori_loop(start, stop, step, 0)


def gather_kernel(n, x_ref, gain_ref, out_ref, own, send, recv, fsend, frecv, local):
    me = lax.axis_index("narrow")
    core = lax.rem(me, 2)
    chip = me // 2
    chips = n // 2
    sibling = me + 1 - 2 * core
    barrier = greet(n, me)
    values = x_ref[...].astype(jnp.float32)
    center = values - jnp.mean(values, axis=-1, keepdims=True)
    spread = jnp.mean(center * center, axis=-1, keepdims=True)
    own[...] = (center * lax.rsqrt(spread + EPSILON) * gain_ref[...]).astype(jnp.bfloat16)
    pl.semaphore_wait(barrier, n - 1)

    def across(k):
        to = lax.rem(chip + k, chips) * 2 + core
        return remote(own, out_ref.at[me], send.at[k], recv.at[k], to)

    def arrived(k):
        return lax.rem(chip - k + chips, chips) * 2 + core

    def forward(k):
        src = arrived(k)
        return remote(out_ref.at[src], out_ref.at[src], fsend.at[k], frecv.at[k], sibling)

    each(1, chips, lambda k: across(k).start())
    first = remote(own, out_ref.at[me], fsend.at[0], frecv.at[0], sibling)
    first.start()
    keep = pltpu.make_async_copy(own, out_ref.at[me], local)
    keep.start()

    def relay(k):
        src = arrived(k)
        remote(own, out_ref.at[src], send.at[k], recv.at[k], sibling).wait_recv()
        forward(k).start()

    each(1, chips, relay)
    keep.wait()

    def finish(k):
        src = lax.rem(chip - k + chips, chips) * 2 + 1 - core
        remote(own, out_ref.at[src], fsend.at[k], frecv.at[k], sibling).wait_recv()

    each(0, chips, finish)
    first.wait_send()
    each(1, chips, lambda k: across(k).wait_send())
    each(1, chips, lambda k: forward(k).wait_send())


def gather_rows(n, rows, gain):
    height, width = rows.shape
    dma = pltpu.SemaphoreType.DMA
    return pl.pallas_call(
        functools.partial(gather_kernel, n),
        out_shape=jax.ShapeDtypeStruct((n, height, width), jnp.bfloat16),
        in_specs=[VMEM, VMEM],
        out_specs=VMEM,
        scratch_shapes=[
            pltpu.VMEM((height, width), jnp.bfloat16),
            dma((n // 2,)),
            dma((n // 2,)),
            dma((n // 2,)),
            dma((n // 2,)),
            dma,
        ],
        compiler_params=pltpu.CompilerParams(
            collective_id=0, has_side_effects=True, vmem_limit_bytes=LIMIT
        ),
    )(rows, gain)


def spread_out(n, me, src, dst, send, recv, local):
    def copy(k):
        peer = lax.rem(me + k, n)
        return remote(src.at[peer], dst.at[me], send.at[k], recv.at[k], peer)

    each(1, n, lambda k: copy(k).start())
    keep = pltpu.make_async_copy(src.at[me], dst.at[me], local)
    keep.start()

    def finish():
        keep.wait()

        def take(k):
            peer = lax.rem(me - k + n, n)
            remote(src.at[peer], dst.at[peer], send.at[k], recv.at[k], peer).wait_recv()

        each(1, n, take)
        each(1, n, lambda k: copy(k).wait_send())

    return finish


def query_kernel(
    n, q_ref, kv_ref, qout_ref, kvout_ref, parts, own, qs, qr, ks, kr, bs, br, local
):
    me = lax.axis_index("narrow")
    barrier = greet(n, me)
    pl.semaphore_wait(barrier, n - 1)
    finish_kv = spread_out(n, me, kv_ref, parts, ks, kr, local.at[0])
    finish_q = spread_out(n, me, q_ref, qout_ref, qs, qr, local.at[1])
    finish_kv()
    own[...] = jnp.sum(parts[...], axis=0).astype(jnp.bfloat16)

    def copy(k):
        peer = lax.rem(me + k, n)
        return remote(own, kvout_ref.at[me], bs.at[k], br.at[k], peer)

    each(1, n, lambda k: copy(k).start())
    keep = pltpu.make_async_copy(own, kvout_ref.at[me], local.at[2])
    keep.start()
    finish_q()
    keep.wait()

    def take(k):
        peer = lax.rem(me - k + n, n)
        remote(own, kvout_ref.at[peer], bs.at[k], br.at[k], peer).wait_recv()

    each(1, n, take)
    each(1, n, lambda k: copy(k).wait_send())


def exchange_queries(n, queries, partial):
    dma = pltpu.SemaphoreType.DMA
    return pl.pallas_call(
        functools.partial(query_kernel, n),
        out_shape=(
            jax.ShapeDtypeStruct(queries.shape, jnp.bfloat16),
            jax.ShapeDtypeStruct(partial.shape, jnp.bfloat16),
        ),
        in_specs=[VMEM, VMEM],
        out_specs=(VMEM, VMEM),
        scratch_shapes=[
            pltpu.VMEM(partial.shape, jnp.float32),
            pltpu.VMEM(partial.shape[1:], jnp.bfloat16),
        ]
        + [dma((n,))] * 6
        + [dma((3,))],
        compiler_params=pltpu.CompilerParams(
            collective_id=1, has_side_effects=True, vmem_limit_bytes=LIMIT
        ),
    )(queries, partial)


def attend_kernel(steps, height, local_heads, info_ref, q_ref, cache_ref, new_ref, out_ref):
    live, chosen, me = info_ref[0], info_ref[1], info_ref[2]
    queries = q_ref[...]
    count = queries.shape[0]
    scale = HEAD_DIM ** (-0.5)

    def scores_of(ref):
        return scale * lax.dot_general(
            queries,
            ref[:, :HEAD_DIM],
            (((1,), (1,)), ((), ())),
            preferred_element_type=jnp.float32,
        )

    row = lax.broadcasted_iota(jnp.int32, (count, 1), 0)
    token = lax.rem(row, height * local_heads) // local_heads
    limit = jnp.where(token < steps, live, 0)
    depth = cache_ref.shape[0]
    position = lax.broadcasted_iota(jnp.int32, (count, depth), 1)
    old = jnp.where(position < limit, scores_of(cache_ref), -1e30)
    fresh_count = new_ref.shape[0]
    column = lax.broadcasted_iota(jnp.int32, (count, fresh_count), 1)
    owner = column // height
    kind = lax.rem(column, height)
    reach = jnp.where(token < steps, jnp.where(chosen > 0, fresh_count, -1), me)
    from_prefill = (kind == steps) & (owner <= reach)
    from_steps = (kind < steps) & (kind <= token) & (token < steps) & (owner == me)
    new = jnp.where(from_prefill | from_steps, scores_of(new_ref), -1e30)
    highest = jnp.maximum(
        jnp.max(old, axis=-1, keepdims=True), jnp.max(new, axis=-1, keepdims=True)
    )
    old = jnp.exp(old - highest)
    new = jnp.exp(new - highest)
    total = jnp.sum(old, axis=-1, keepdims=True) + jnp.sum(new, axis=-1, keepdims=True)
    mixed = jnp.dot(
        old.astype(jnp.bfloat16), cache_ref[:, HEAD_DIM:], preferred_element_type=jnp.float32
    )
    mixed = mixed + jnp.dot(
        new.astype(jnp.bfloat16), new_ref[:, HEAD_DIM:], preferred_element_type=jnp.float32
    )
    out_ref[...] = (mixed / total).astype(jnp.bfloat16)


def attend(steps, height, local_heads, info, queries, cache, new):
    return pl.pallas_call(
        functools.partial(attend_kernel, steps, height, local_heads),
        out_shape=jax.ShapeDtypeStruct(queries.shape, jnp.bfloat16),
        in_specs=[SMEM, VMEM, VMEM, VMEM],
        out_specs=VMEM,
        compiler_params=pltpu.CompilerParams(vmem_limit_bytes=LIMIT),
    )(info, queries, cache, new)


def mixed_kernel(n, x_ref, out_ref, send, recv, local):
    me = lax.axis_index("narrow")
    barrier = greet(n, me)
    pl.semaphore_wait(barrier, n - 1)
    spread_out(n, me, x_ref, out_ref, send, recv, local)()


def exchange_mixed(n, mixed):
    dma = pltpu.SemaphoreType.DMA
    return pl.pallas_call(
        functools.partial(mixed_kernel, n),
        out_shape=jax.ShapeDtypeStruct(mixed.shape, mixed.dtype),
        in_specs=[VMEM],
        out_specs=VMEM,
        scratch_shapes=[dma((n,)), dma((n,)), dma],
        compiler_params=pltpu.CompilerParams(
            collective_id=2, has_side_effects=True, vmem_limit_bytes=LIMIT
        ),
    )(mixed)


def reduce_kernel(n, x_ref, out_ref, near, pair, far, psend, precv, send, recv):
    me = lax.axis_index("narrow")
    core = lax.rem(me, 2)
    chip = me // 2
    chips = n // 2
    sibling = me + 1 - 2 * core
    barrier = greet(n, me)
    pl.semaphore_wait(barrier, n - 1)

    def target(k):
        return lax.rem(chip + k, chips)

    def swap(k):
        return remote(
            x_ref.at[target(k) * 2 + 1 - core],
            near.at[k],
            psend.at[k],
            precv.at[k],
            sibling,
        )

    def across(k):
        return remote(
            pair.at[k], far.at[k], send.at[k], recv.at[k], target(k) * 2 + core
        )

    each(1, chips, lambda k: swap(k).start())
    swap(0).start()

    def both(k):
        swap(k).wait_recv()
        return x_ref[target(k) * 2 + core].astype(jnp.float32) + near[k].astype(jnp.float32)

    def relay(k):
        pair[k] = both(k).astype(jnp.bfloat16)
        across(k).start()

    each(1, chips, relay)
    total = both(0)

    def add(k, total):
        across(k).wait_recv()
        return total + far[k].astype(jnp.float32)

    for k in range(1, chips):
        total = add(k, total)
    out_ref[...] = total.astype(jnp.bfloat16)
    each(0, chips, lambda k: swap(k).wait_send())
    each(1, chips, lambda k: across(k).wait_send())


def reduce_rows(n, partial):
    dma = pltpu.SemaphoreType.DMA
    half = (n // 2,) + partial.shape[1:]
    return pl.pallas_call(
        functools.partial(reduce_kernel, n),
        out_shape=jax.ShapeDtypeStruct(partial.shape[1:], jnp.bfloat16),
        in_specs=[VMEM],
        out_specs=VMEM,
        scratch_shapes=[pltpu.VMEM(half, jnp.bfloat16)] * 3 + [dma((n // 2,))] * 4,
        compiler_params=pltpu.CompilerParams(
            collective_id=3, has_side_effects=True, vmem_limit_bytes=LIMIT
        ),
    )(partial)


def per_device(
    prefill_rows,
    decode_rows,
    kv_cache,
    slot_lengths,
    prefill_slot,
    norm_gain,
    query_weight,
    keyval_weight,
    output_weight,
):
    n = lax.axis_size("narrow")
    rank = lax.axis_index("narrow")
    steps = decode_rows.shape[1]
    assert decode_rows.shape[0] == 1 and prefill_rows.shape[0] == 1
    height = steps + 1
    width = prefill_rows.shape[1]
    heads = query_weight.shape[0] // HEAD_DIM
    columns = query_weight.shape[1]
    depth = keyval_weight.shape[0]
    rows = jnp.concatenate([decode_rows[0], prefill_rows], axis=0)
    normed = gather_rows(n, rows, norm_gain[None])
    flat = normed.reshape(n * height, width)
    queries = jnp.dot(flat, query_weight, preferred_element_type=jnp.float32)
    queries = queries.astype(jnp.bfloat16)
    part = lax.dynamic_slice_in_dim(flat, rank * depth, depth, 1)
    partial = jnp.dot(part, keyval_weight, preferred_element_type=jnp.float32)
    whole_heads = columns % HEAD_DIM == 0
    if whole_heads:
        local_heads = columns // HEAD_DIM
        block = (n, height * local_heads, HEAD_DIM)
    else:
        local_heads = heads
        block = (n, height, columns)
    queries, new = exchange_queries(
        n, queries.reshape(block), partial.reshape(n, height, 2 * HEAD_DIM)
    )
    if not whole_heads:
        queries = queries.transpose(1, 0, 2)
    chosen = rank == prefill_slot[0]
    live = jnp.where(chosen, 0, slot_lengths[0])
    info = jnp.stack([live, chosen.astype(jnp.int32), rank.astype(jnp.int32)])
    mixed = attend(
        steps,
        height,
        local_heads,
        info,
        queries.reshape(height * heads, HEAD_DIM),
        kv_cache[0],
        new.reshape(n * height, 2 * HEAD_DIM),
    )
    if not whole_heads:
        mixed = mixed.reshape(height, n, columns).transpose(1, 0, 2)
    mixed = exchange_mixed(n, mixed.reshape(block))
    partial = jnp.dot(
        mixed.reshape(n * height, columns), output_weight, preferred_element_type=jnp.float32
    )
    out = reduce_rows(n, partial.astype(jnp.bfloat16).reshape(n, height, width))
    return (out[steps:], out[None, :steps])


def solution(mesh):
    in_specs = (
        P(("group", "narrow"), None),
        P(("group", "narrow"), None, None),
        P(("group", "narrow"), None, None),
        P(("group", "narrow")),
        P("group"),
        P(),
        P(None, "narrow"),
        P("narrow", None),
        P("narrow", None),
    )
    out_specs = (P(("group", "narrow"), None), P(("group", "narrow"), None, None))
    return jax.shard_map(
        per_device, mesh=mesh, in_specs=in_specs, out_specs=out_specs, check_vma=False
    )
```

time: 293 us -> 64.1 us (0.22)
  blocking collectives: 178 us -> 0 us
  Pallas kernels: 0 us -> 51.4 us
  other arithmetic: 45.4 us -> 0.95 us
  local copies, waits for them, and re-layouts: 21.1 us -> 2.63 us
  starting transfers between devices: 14.2 us -> 0 us
  waiting for transfers between devices: 13.7 us -> 0 us
  matrix products: 16.7 us -> 6.62 us
    unnamed x1 -> x0, blocking collectives: 71.9 us -> none
    psum x1 -> x0, blocking collectives: 57.9 us -> none  [per_device(): keyvals = lax.psum(partial_kv, 'narrow').astype(jnp.bfloat16)]
    pallas_call x0 -> x5, Pallas kernels: none -> 51.4 us  [the longest x1 16.1 us: exchange_queries(): pl.pallas_call(functools.partial(query_kernel, n), out_shape=(jax.ShapeDt...]
    all_gather x2 -> x0, blocking collectives: 48.6 us -> none  [the longest x1 24.5 us: per_device(): gathered = lax.all_gather(prefill_rows, 'narrow', axis=0, tiled=True)]
    unnamed x5 -> x0, other arithmetic: 35.2 us -> none
    all_to_all x4 -> x0, starting transfers between devices: 14.2 us -> none  [the longest x1 3.68 us: per_device(): lax.all_to_all(query_local, 'narrow', split_axis=0, concat_axis=2, tiled=...]
    all_to_all x4 -> x0, waiting for transfers between devices: 13.7 us -> none  [the longest x1 6.44 us: per_device(): lax.all_to_all(query_local, 'narrow', split_axis=0, concat_axis=2, tiled=...]
    dot_general x18 -> x3, matrix products: 16.7 us -> 6.62 us  [the longest x1 3.29 us: per_device(): jnp.dot(mixed.reshape(n * height, columns), output_weight, preferred_elem...]
  transfers between devices with their start and end apart: 4 -> 0, of which waited for: 3 -> 0; matrix products, arithmetic and copies ran while one was open for 4% -> 0% of each run, Pallas kernels for 0% -> 0%
where the time goes in v1:
time: 64.1 us; the launch traced here: 63.8 us
  Pallas kernels  51.4 us (80%)
  matrix products  6.62 us (10%)
  local copies, waits for them, and re-layouts  2.63 us (4%)
  between operations  2.18 us (3%)
  other arithmetic  0.95 us (1%)
    pallas_call x1, Pallas kernels, exchange_queries(): pl.pallas_call(functools.partial(query_kernel, n), out_shape=(jax.ShapeDt...  16.1 us
    pallas_call x1, Pallas kernels, gather_rows(): pl.pallas_call(functools.partial(gather_kernel, n), out_shape=jax.ShapeDt...  14.3 us
    pallas_call x1, Pallas kernels, reduce_rows(): pl.pallas_call(functools.partial(reduce_kernel, n), out_shape=jax.ShapeDt...  12.3 us
    pallas_call x1, Pallas kernels, exchange_mixed(): pl.pallas_call(functools.partial(mixed_kernel, n), out_shape=jax.ShapeDty...  6.99 us
    dot_general x1, matrix products, per_device(): jnp.dot(mixed.reshape(n * height, columns), output_weight, preferred_elem...  3.29 us
    dot_general x1, matrix products, per_device(): queries = jnp.dot(flat, query_weight, preferred_element_type=jnp.float32)  3.17 us
    pallas_call x1, Pallas kernels, attend(): pl.pallas_call(functools.partial(attend_kernel, steps, height, local_head...  1.63 us

profile of v1, /device:TPU:0, one launch (start us, length us, event | category | flops | bytes accessed | tf_op | source)
XLA Modules:
  0.0 63.8 jit_solution(15850597479544071472)
XLA Ops:
  0.6 0.0 copy-start
  0.6 0.0 copy-start.1
  2.1 0.1 pad_add_fusion.info_ref
  2.1 0.9 %pad_maximum_fusion.x_ref = bf16[4,6144]{1,0:T(4,128)(2,1)S(1)} fusion(bf16[1,6144]{1,0:T(2,128)(2,1)} %param.9, bf16[3,6144]{1,0:T(4,128)(2,1)} %bitcast.19), kind=kLoop, calls=%fused_computation.2 | loop fusion | flops 98304 | bytes 98304 | tf_op jit(solution)/shard_map/concatenate | solution.py:352
  3.0 0.0 copy-start.2
  3.0 0.7 %copy-done.2 = f32[6144]{0:T(1024)S(1)} copy-done((f32[6144]{0:T(1024)S(1)}, f32[6144]{0:T(1024)}, u32[]{:S(2)}) %copy-start.2) | copy-done | bytes 24600
  3.7 14.3 %shard_map.104 = bf16[16,4,6144]{2,1,0:T(4,128)(2,1)S(1)} custom-call(bf16[4,6144]{1,0:T(4,128)(2,1)S(1)} %pad_maximum_fusion.x_ref, f32[1,6144]{1,0:T(1,128)S(1)} %bitcast.18), custom_call_target="tpu_custom_call" | custom-call | tf_op jit(solution)/shard_map/pallas_call | solution.py:100
  18.1 0.2 reshape.28
  18.3 3.2 %convolution_convert_fusion.1 = bf16[64,384]{1,0:T(8,128)(2,1)S(1)} fusion(bf16[64,6144]{1,0:T(8,128)(2,1)S(1)} %reshape.28, bf16[6144,384]{1,0:T(8,128)(2,1)} %param.15), kind=kOutput, calls=%fused_computation.1 | convolution fusion | flops 302014464 | bytes 5554176 | tf_op jit(solution)/shard_map/dot_general | solution.py:355
  21.5 0.0 copy-done
  21.5 0.2 fusion
  21.7 16.1 %shard_map.105 = (bf16[16,12,128]{2,1,0:T(8,128)(2,1)S(1)}, bf16[16,4,256]{2,1,0:T(4,128)(2,1)S(1)}) custom-call(bf16[16,12,128]{2,1,0:T(8,128)(2,1)S(1)} %reshape.29.q_ref, f32[16,4,256]{2,1,0:T(4,128)S(1)} %reshape.30.kv_ref), custom_call_target="tpu_custom_call" | custom-call | tf_op jit(solution)/shard_map/pallas_call | solution.py:172
  37.9 0.0 copy-done.1
  37.9 1.6 %shard_map.106 = bf16[192,128]{1,0:T(8,128)(2,1)S(1)} custom-call(s32[3]{0:T(128)S(1)} %pad_add_fusion.info_ref, bf16[192,128]{1,0:T(8,128)(2,1)S(1)} %reshape.31.q_ref, bf16[2048,256]{1,0:T(8,128)(2,1)S(1)} %bitcast.17, bf16[64,256]{1,0:T(8,128)(2,1)S(1)} %reshape.32.new_ref), custom_call_target="tpu_custom_call" | custom-call | tf_op jit(solution)/shard_map/pallas_call | solution.py:236
  39.5 7.0 %shard_map.107 = bf16[16,12,128]{2,1,0:T(8,128)(2,1)S(1)} custom-call(bf16[16,12,128]{2,1,0:T(8,128)(2,1)S(1)} %reshape.33.x_ref), custom_call_target="tpu_custom_call" | custom-call | tf_op jit(solution)/shard_map/pallas_call | solution.py:254
  46.6 3.3 %convolution_convert_fusion = bf16[64,6144]{1,0:T(8,128)(2,1)S(1)} fusion(bf16[64,384]{1,0:T(8,128)(2,1)S(1)} %reshape.34, bf16[384,6144]{1,0:T(8,128)(2,1)} %param.17), kind=kOutput, calls=%fused_computation | convolution fusion | flops 302383104 | bytes 5554176 | tf_op jit(solution)/shard_map/dot_general | solution.py:386
  49.9 0.3 reshape.35.x_ref
  50.2 12.3 %shard_map.108 = bf16[4,6144]{1,0:T(4,128)(2,1)S(1)} custom-call(bf16[16,4,6144]{2,1,0:T(4,128)(2,1)S(1)} %reshape.35.x_ref), custom_call_target="tpu_custom_call" | custom-call | tf_op jit(solution)/shard_map/pallas_call | solution.py:320
  62.5 0.6 slice.6
  63.2 0.6 slice_bitcast_fusion
  (6 shorter events, 0.1 us)
Async XLA Ops:
  0.6 20.8 %copy-start = (bf16[384,256]{1,0:T(8,128)(2,1)S(1)}, bf16[384,256]{1,0:T(8,128)(2,1)}, u32[]{:S(2)}) copy-start(bf16[384,256]{1,0:T(8,128)(2,1)} %param.16) | copy-start | bytes 589828
  0.6 37.2 %copy-start.1 = (bf16[1,2048,256]{2,1,0:T(8,128)(2,1)S(1)}, bf16[1,2048,256]{2,1,0:T(8,128)(2,1)}, u32[]{:S(2)}) copy-start(bf16[1,2048,256]{2,1,0:T(8,128)(2,1)} %param.11) | copy-start | bytes 3145732
  3.0 0.7 %copy-start.2 = (f32[6144]{0:T(1024)S(1)}, f32[6144]{0:T(1024)}, u32[]{:S(2)}) copy-start(f32[6144]{0:T(1024)} %param.14) | copy-start | bytes 73732

commit v2 on v1

--- a/solution.py
+++ b/solution.py
@@ -329,6 +329,321 @@
     )(partial)
 
 
+def fused_kernel(
+    n,
+    steps,
+    local_heads,
+    length_ref,
+    slot_ref,
+    prefill_ref,
+    decode_ref,
+    gain_ref,
+    cache_hbm,
+    wq_hbm,
+    wkv_hbm,
+    wo_hbm,
+    pre_out,
+    dec_out,
+    cache,
+    wq,
+    wkv,
+    wo,
+    own,
+    rows,
+    q_from,
+    q_to,
+    kv_from,
+    kv_to,
+    kv_own,
+    new_ref,
+    mix_from,
+    mix_to,
+    part,
+    near,
+    pair,
+    far,
+    load,
+    gs,
+    gr,
+    fs,
+    fr,
+    qs,
+    qr,
+    ks,
+    kr,
+    bs,
+    br,
+    ms,
+    mr,
+    ps,
+    pr,
+    ss,
+    sr,
+):
+    me = lax.axis_index("narrow")
+    core = lax.rem(me, 2)
+    chip = me // 2
+    chips = n // 2
+    sibling = me + 1 - 2 * core
+    chunks, height, wide = own.shape
+    depth = wkv.shape[0]
+    columns = wq.shape[1]
+    barrier = greet(n, me)
+    loads = [
+        pltpu.make_async_copy(src, dst, load.at[i])
+        for i, (src, dst) in enumerate(
+            ((wq_hbm, wq), (wkv_hbm, wkv), (cache_hbm, cache), (wo_hbm, wo))
+        )
+    ]
+    for copy in loads:
+        copy.start()
+    values = jnp.concatenate(
+        [decode_ref[...].astype(jnp.float32), prefill_ref[...].astype(jnp.float32)], axis=0
+    )
+    center = values - jnp.mean(values, axis=-1, keepdims=True)
+    spread = jnp.mean(center * center, axis=-1, keepdims=True)
+    normed = (center * lax.rsqrt(spread + EPSILON) * gain_ref[...]).astype(jnp.bfloat16)
+    for c in range(chunks):
+        own[c] = normed[:, c * wide : (c + 1) * wide]
+        rows[c, me] = normed[:, c * wide : (c + 1) * wide]
+    pl.semaphore_wait(barrier, n - 1)
+
+    def target(k):
+        return lax.rem(chip + k, chips)
+
+    def source(k):
+        return lax.rem(chip - k + chips, chips)
+
+    def across(c, k):
+        to = target(k) * 2 + core
+        return remote(own.at[c], rows.at[c, me], gs.at[c, k], gr.at[c, k], to)
+
+    def first(c):
+        return remote(own.at[c], rows.at[c, me], fs.at[c, 0], fr.at[c, 0], sibling)
+
+    def forward(c, k):
+        block = rows.at[c, source(k) * 2 + core]
+        return remote(block, block, fs.at[c, k], fr.at[c, k], sibling)
+
+    for c in range(chunks):
+        each(1, chips, lambda k: across(c, k).start())
+        first(c).start()
+
+    def relay(c):
+        def step(k):
+            block = rows.at[c, source(k) * 2 + core]
+            remote(own.at[c], block, gs.at[c, k], gr.at[c, k], sibling).wait_recv()
+            forward(c, k).start()
+
+        each(1, chips, step)
+
+    def gathered(c):
+        def step(k):
+            block = rows.at[c, source(k) * 2 + 1 - core]
+            remote(own.at[c], block, fs.at[c, k], fr.at[c, k], sibling).wait_recv()
+
+        each(0, chips, step)
+
+    def project(c):
+        return jnp.dot(
+            rows[c].reshape(n * height, wide),
+            wq[c * wide : (c + 1) * wide, :],
+            preferred_element_type=jnp.float32,
+        )
+
+    def start_all(src, dst, send, recv):
+        def copy(k):
+            peer = lax.rem(me + k, n)
+            block = src.at[peer] if len(src.shape) == len(dst.shape) else src
+            return remote(block, dst.at[me], send.at[k], recv.at[k], peer)
+
+        each(1, n, lambda k: copy(k).start())
+
+        def arrive():
+            def take(k):
+                peer = lax.rem(me - k + n, n)
+                block = src.at[peer] if len(src.shape) == len(dst.shape) else src
+                remote(block, dst.at[peer], send.at[k], recv.at[k], peer).wait_recv()
+
+            each(1, n, take)
+
+        return arrive, lambda: each(1, n, lambda k: copy(k).wait_send())
+
+    relay(0)
+    queries = jnp.zeros((n * height, columns), jnp.float32)
+    for c in range(chunks):
+        if c + 1 < chunks:
+            relay(c + 1)
+        gathered(c)
+        if c == 0:
+            loads[0].wait()
+        if c + 1 == chunks:
+            loads[1].wait()
+            share = n // chunks
+            start = pl.multiple_of(lax.rem(me, share) * depth, 128)
+            piece = rows[me // share, :, :, pl.ds(start, depth)].reshape(n * height, depth)
+            partial = jnp.dot(piece, wkv[...], preferred_element_type=jnp.float32)
+            kv_from[...] = partial.reshape(n, height, 2 * HEAD_DIM)
+            kv_to[me] = kv_from[me]
+            kv_arrive, kv_sent = start_all(kv_from, kv_to, ks, kr)
+        queries = queries + project(c)
+    q_from[...] = queries.reshape(n, height * local_heads, HEAD_DIM).astype(jnp.bfloat16)
+    q_to[me] = q_from[me]
+    q_arrive, q_sent = start_all(q_from, q_to, qs, qr)
+    kv_arrive()
+    fresh = jnp.sum(kv_to[...], axis=0).astype(jnp.bfloat16)
+    kv_own[...] = fresh
+    new_ref[me] = fresh
+    new_arrive, new_sent = start_all(kv_own, new_ref, bs, br)
+    q_arrive()
+
+    block_rows = height * local_heads
+    count = n * block_rows
+    own_queries = q_to[...].reshape(count, HEAD_DIM)
+    scale = HEAD_DIM ** (-0.5)
+
+    def scores_of(keys):
+        return scale * lax.dot_general(
+            own_queries, keys, (((1,), (1,)), ((), ())), preferred_element_type=jnp.float32
+        )
+
+    chosen = slot_ref[0] == me
+    live = jnp.where(chosen, 0, length_ref[0])
+    token = lax.rem(lax.broadcasted_iota(jnp.int32, (count, 1), 0), block_rows) // local_heads
+    limit = jnp.where(token < steps, live, 0)
+    loads[2].wait()
+    position = lax.broadcasted_iota(jnp.int32, (count, cache.shape[0]), 1)
+    old = jnp.where(position < limit, scores_of(cache[:, :HEAD_DIM]), -1e30)
+    highest = jnp.max(old, axis=-1, keepdims=True)
+    new_arrive()
+    keyvals = new_ref[...].reshape(n * height, 2 * HEAD_DIM)
+    column = lax.broadcasted_iota(jnp.int32, (count, n * height), 1)
+    owner = column // height
+    kind = lax.rem(column, height)
+    reach = jnp.where(token < steps, jnp.where(chosen, n, -1), me)
+    from_prefill = (kind == steps) & (owner <= reach)
+    from_steps = (kind < steps) & (kind <= token) & (token < steps) & (owner == me)
+    new = jnp.where(from_prefill | from_steps, scores_of(keyvals[:, :HEAD_DIM]), -1e30)
+    highest = jnp.maximum(highest, jnp.max(new, axis=-1, keepdims=True))
+    old = jnp.exp(old - highest)
+    new = jnp.exp(new - highest)
+    total = jnp.sum(old, axis=-1, keepdims=True) + jnp.sum(new, axis=-1, keepdims=True)
+    mixed = jnp.dot(
+        old.astype(jnp.bfloat16), cache[:, HEAD_DIM:], preferred_element_type=jnp.float32
+    )
+    mixed = mixed + jnp.dot(
+        new.astype(jnp.bfloat16), keyvals[:, HEAD_DIM:], preferred_element_type=jnp.float32
+    )
+    mix_from[...] = (mixed / total).reshape(n, block_rows, HEAD_DIM).astype(jnp.bfloat16)
+    mix_to[me] = mix_from[me]
+    mix_arrive, mix_sent = start_all(mix_from, mix_to, ms, mr)
+    loads[3].wait()
+    mix_arrive()
+    flat = mix_to[...].astype(jnp.float32).reshape(n * height, columns).astype(jnp.bfloat16)
+
+    def swap(e):
+        return remote(part.at[e, 1 - core], near.at[e], ps.at[e], pr.at[e], sibling)
+
+    def out_across(e, k):
+        to = target(k)
+        return remote(
+            pair.at[e, to], far.at[e, chip], ss.at[e, k], sr.at[e, k], to * 2 + core
+        )
+
+    def fold(e):
+        swap(e).wait_recv()
+        both = part[e, core].astype(jnp.float32) + near[e].astype(jnp.float32)
+        pair[e] = both.astype(jnp.bfloat16)
+        each(1, chips, lambda k: out_across(e, k).start())
+        far[e, chip] = pair[e, chip]
+
+    for e in range(chunks):
+        product = jnp.dot(
+            flat, wo[:, e * wide : (e + 1) * wide], preferred_element_type=jnp.float32
+        )
+        product = product.reshape(chips, 2, height, wide).astype(jnp.bfloat16)
+        part[e, 0] = product[:, 0]
+        part[e, 1] = product[:, 1]
+        swap(e).start()
+        if e > 0:
+            fold(e - 1)
+    fold(chunks - 1)
+    for e in range(chunks):
+
+        def take(k):
+            remote(
+                pair.at[e, 0], far.at[e, source(k)], ss.at[e, k], sr.at[e, k], sibling
+            ).wait_recv()
+
+        each(1, chips, take)
+        result = jnp.sum(far[e].astype(jnp.float32), axis=0).astype(jnp.bfloat16)
+        dec_out[:, e * wide : (e + 1) * wide] = result[:steps]
+        pre_out[:, e * wide : (e + 1) * wide] = result[steps:]
+    for c in range(chunks):
+        each(1, chips, lambda k: across(c, k).wait_send())
+        first(c).wait_send()
+        each(1, chips, lambda k: forward(c, k).wait_send())
+        swap(c).wait_send()
+        each(1, chips, lambda k: out_across(c, k).wait_send())
+    kv_sent()
+    q_sent()
+    new_sent()
+    mix_sent()
+
+
+def fused(n, prefill, decode, cache, length, slot, gain, wq, wkv, wo):
+    dma = pltpu.SemaphoreType.DMA
+    steps, width = decode.shape
+    height = steps + 1
+    columns = wq.shape[1]
+    local_heads = columns // HEAD_DIM
+    chunks = 4
+    wide = width // chunks
+    chips = n // 2
+    heads_block = (n, height * local_heads, HEAD_DIM)
+    new_block = (n, height, 2 * HEAD_DIM)
+    half = (chunks, chips, height, wide)
+    narrow = jnp.bfloat16
+    hbm = pl.BlockSpec(memory_space=pltpu.HBM)
+    return pl.pallas_call(
+        functools.partial(fused_kernel, n, steps, local_heads),
+        out_shape=(
+            jax.ShapeDtypeStruct(prefill.shape, narrow),
+            jax.ShapeDtypeStruct(decode.shape, narrow),
+        ),
+        in_specs=[SMEM, SMEM, VMEM, VMEM, VMEM, hbm, hbm, hbm, hbm],
+        out_specs=(VMEM, VMEM),
+        scratch_shapes=[
+            pltpu.VMEM(cache.shape, narrow),
+            pltpu.VMEM(wq.shape, narrow),
+            pltpu.VMEM(wkv.shape, narrow),
+            pltpu.VMEM(wo.shape, narrow),
+            pltpu.VMEM((chunks, height, wide), narrow),
+            pltpu.VMEM((chunks, n, height, wide), narrow),
+            pltpu.VMEM(heads_block, narrow),
+            pltpu.VMEM(heads_block, narrow),
+            pltpu.VMEM(new_block, jnp.float32),
+            pltpu.VMEM(new_block, jnp.float32),
+            pltpu.VMEM(new_block[1:], narrow),
+            pltpu.VMEM(new_block, narrow),
+            pltpu.VMEM(heads_block, narrow),
+            pltpu.VMEM(heads_block, narrow),
+            pltpu.VMEM((chunks, 2, chips, height, wide), narrow),
+            pltpu.VMEM(half, narrow),
+            pltpu.VMEM(half, narrow),
+            pltpu.VMEM(half, narrow),
+            dma((4,)),
+        ]
+        + [dma((chunks, chips))] * 4
+        + [dma((n,))] * 8
+        + [dma((chunks,))] * 2
+        + [dma((chunks, chips))] * 2,
+        compiler_params=pltpu.CompilerParams(
+            collective_id=4, has_side_effects=True, vmem_limit_bytes=48 * 1024 * 1024
+        ),
+    )(length, slot, prefill, decode, gain, cache, wq, wkv, wo)
+
+
 def per_device(
     prefill_rows,
     decode_rows,
@@ -349,6 +664,20 @@
     heads = query_weight.shape[0] // HEAD_DIM
     columns = query_weight.shape[1]
     depth = keyval_weight.shape[0]
+    if columns % HEAD_DIM == 0 and n % 4 == 0 and depth % HEAD_DIM == 0:
+        prefill_out, decode_out = fused(
+            n,
+            prefill_rows,
+            decode_rows[0],
+            kv_cache[0],
+            slot_lengths,
+            prefill_slot,
+            norm_gain[None],
+            query_weight,
+            keyval_weight,
+            output_weight,
+        )
+        return (prefill_out, decode_out[None])
     rows = jnp.concatenate([decode_rows[0], prefill_rows], axis=0)
     normed = gather_rows(n, rows, norm_gain[None])
     flat = normed.reshape(n * height, width)

time: 64.1 us -> 56.6 us (0.88)
  matrix products: 6.62 us -> 0 us
  local copies, waits for them, and re-layouts: 2.63 us -> 7.98 us
  Pallas kernels: 51.4 us -> 46.3 us
  other arithmetic: 0.95 us -> 0 us
    unnamed x6 -> x14, local copies, waits for them, and re-layouts: 0.75 us -> 7.98 us
    dot_general x3 -> x0, matrix products: 6.62 us -> none  [the longest x1 3.29 us: per_device(): jnp.dot(mixed.reshape(n * height, columns), output_weight, preferred_elem...]
    pallas_call x5 -> x1, Pallas kernels: 51.4 us -> 46.3 us  [fused(): pl.pallas_call(functools.partial(fused_kernel, n, steps, local_heads), ou...]
    concatenate x1 -> x0, other arithmetic: 0.87 us -> none  [per_device(): rows = jnp.concatenate([decode_rows[0], prefill_rows], axis=0)]
where the time goes in v2:
time: 56.6 us; the launch traced here: 56.2 us
  Pallas kernels  46.3 us (82%)
  local copies, waits for them, and re-layouts  7.98 us (14%)
  between operations  1.95 us (3%)
    pallas_call x1, Pallas kernels, fused(): pl.pallas_call(functools.partial(fused_kernel, n, steps, local_heads), ou...  46.3 us
    unnamed x14, local copies, waits for them, and re-layouts  7.98 us

profile of v2, /device:TPU:0, one launch (start us, length us, event | category | flops | bytes accessed | tf_op | source)
XLA Modules:
  0.0 56.2 jit_solution(14964421150144600452)
XLA Ops:
  1.9 0.0 copy-start
  1.9 2.3 %copy-done = bf16[6144,384]{1,0:T(8,128)(2,1)S(1)} copy-done((bf16[6144,384]{1,0:T(8,128)(2,1)S(1)}, bf16[6144,384]{1,0:T(8,128)(2,1)}, u32[]{:S(2)}) %copy-start) | copy-done | bytes 4718616
  4.3 0.0 copy-start.1
  4.3 1.2 %copy-done.1 = bf16[1,2048,256]{2,1,0:T(8,128)(2,1)S(1)} copy-done((bf16[1,2048,256]{2,1,0:T(8,128)(2,1)S(1)}, bf16[1,2048,256]{2,1,0:T(8,128)(2,1)}, u32[]{:S(2)}) %copy-start.1) | copy-done | bytes 1048600
  5.5 0.0 copy-start.2
  5.5 0.9 %copy-done.2 = bf16[384,256]{1,0:T(8,128)(2,1)S(1)} copy-done((bf16[384,256]{1,0:T(8,128)(2,1)S(1)}, bf16[384,256]{1,0:T(8,128)(2,1)}, u32[]{:S(2)}) %copy-start.2) | copy-done | bytes 196632
  6.4 0.0 copy-start.3
  6.4 0.8 %copy-done.3 = bf16[1,3,6144]{2,1,0:T(4,128)(2,1)S(1)} copy-done((bf16[1,3,6144]{2,1,0:T(4,128)(2,1)S(1)}, bf16[1,3,6144]{2,1,0:T(4,128)(2,1)}, u32[]{:S(2)}) %copy-start.3) | copy-done | bytes 36888
  7.2 0.0 copy-start.4
  7.2 0.7 %copy-done.4 = bf16[1,6144]{1,0:T(2,128)(2,1)S(1)} copy-done((bf16[1,6144]{1,0:T(2,128)(2,1)S(1)}, bf16[1,6144]{1,0:T(2,128)(2,1)}, u32[]{:S(2)}) %copy-start.4) | copy-done | bytes 12312
  8.0 0.0 copy-start.5
  8.0 0.7 %copy-done.5 = f32[6144]{0:T(1024)S(1)} copy-done((f32[6144]{0:T(1024)S(1)}, f32[6144]{0:T(1024)}, u32[]{:S(2)}) %copy-start.5) | copy-done | bytes 24600
  8.7 46.3 %shard_map.104 = (bf16[1,6144]{1,0:T(2,128)(2,1)S(1)}, bf16[3,6144]{1,0:T(4,128)(2,1)S(1)}) custom-call(s32[1]{0:T(128)S(6)} %copy.13.length_ref, s32[1]{0:T(128)S(6)} %copy.14.slot_ref, bf16[1,6144]{1,0:T(2,128)(2,1)S(1)} %copy-done.4, bf16[3,6144]{1,0:T(4,128)(2,1)S(1)} %bitcast.5, f32[1,6144]{1,0:T(1,128)S(1)} %bitcast.7, bf16[2048,256]{1,0:T(8,128)(2,1)S(1)} %bitcast.4, ...), custom_call_target="tpu_custom_call" | custom-call | tf_op jit(solution)/shard_map/pallas_call | solution.py:608
  55.0 0.6 %copy.15 = bf16[1,6144]{1,0:T(2,128)(2,1)} copy(bf16[1,6144]{1,0:T(2,128)(2,1)S(1)} %get-tuple-element.8) | data formatting | bytes 24576
  55.6 0.6 %copy.16 = bf16[1,3,6144]{2,1,0:T(4,128)(2,1)} copy(bf16[1,3,6144]{2,1,0:T(4,128)(2,1)S(1)} %bitcast.6) | data formatting | bytes 73728
Async XLA Ops:
  1.9 2.3 %copy-start = (bf16[6144,384]{1,0:T(8,128)(2,1)S(1)}, bf16[6144,384]{1,0:T(8,128)(2,1)}, u32[]{:S(2)}) copy-start(bf16[6144,384]{1,0:T(8,128)(2,1)} %wq_hbm.1) | copy-start | bytes 14155780
  4.3 1.2 %copy-start.1 = (bf16[1,2048,256]{2,1,0:T(8,128)(2,1)S(1)}, bf16[1,2048,256]{2,1,0:T(8,128)(2,1)}, u32[]{:S(2)}) copy-start(bf16[1,2048,256]{2,1,0:T(8,128)(2,1)} %param.11) | copy-start | bytes 3145732
  5.5 0.9 %copy-start.2 = (bf16[384,256]{1,0:T(8,128)(2,1)S(1)}, bf16[384,256]{1,0:T(8,128)(2,1)}, u32[]{:S(2)}) copy-start(bf16[384,256]{1,0:T(8,128)(2,1)} %wkv_hbm.1) | copy-start | bytes 589828
  6.4 0.8 %copy-start.3 = (bf16[1,3,6144]{2,1,0:T(4,128)(2,1)S(1)}, bf16[1,3,6144]{2,1,0:T(4,128)(2,1)}, u32[]{:S(2)}) copy-start(bf16[1,3,6144]{2,1,0:T(4,128)(2,1)} %param.10) | copy-start | bytes 110596
  7.2 0.7 %copy-start.4 = (bf16[1,6144]{1,0:T(2,128)(2,1)S(1)}, bf16[1,6144]{1,0:T(2,128)(2,1)}, u32[]{:S(2)}) copy-start(bf16[1,6144]{1,0:T(2,128)(2,1)} %prefill_ref.1) | copy-start | bytes 36868
  8.0 0.7 %copy-start.5 = (f32[6144]{0:T(1024)S(1)}, f32[6144]{0:T(1024)}, u32[]{:S(2)}) copy-start(f32[6144]{0:T(1024)} %param.14) | copy-start | bytes 73732

commit v3 on v2

--- a/solution.py
+++ b/solution.py
@@ -348,7 +348,6 @@
     wq,
     wkv,
     wo,
-    own,
     rows,
     q_from,
     q_to,
@@ -385,7 +384,7 @@
     chip = me // 2
     chips = n // 2
     sibling = me + 1 - 2 * core
-    chunks, height, wide = own.shape
+    chunks, height, wide = rows.shape[0], rows.shape[3], rows.shape[4]
     depth = wkv.shape[0]
     columns = wq.shape[1]
     barrier = greet(n, me)
@@ -404,45 +403,38 @@
     spread = jnp.mean(center * center, axis=-1, keepdims=True)
     normed = (center * lax.rsqrt(spread + EPSILON) * gain_ref[...]).astype(jnp.bfloat16)
     for c in range(chunks):
-        own[c] = normed[:, c * wide : (c + 1) * wide]
-        rows[c, me] = normed[:, c * wide : (c + 1) * wide]
+        rows[c, core, chip] = normed[:, c * wide : (c + 1) * wide]
     pl.semaphore_wait(barrier, n - 1)
+    place = core * chips + chip
 
     def target(k):
         return lax.rem(chip + k, chips)
 
-    def source(k):
-        return lax.rem(chip - k + chips, chips)
-
     def across(c, k):
-        to = target(k) * 2 + core
-        return remote(own.at[c], rows.at[c, me], gs.at[c, k], gr.at[c, k], to)
-
-    def first(c):
-        return remote(own.at[c], rows.at[c, me], fs.at[c, 0], fr.at[c, 0], sibling)
-
-    def forward(c, k):
-        block = rows.at[c, source(k) * 2 + core]
-        return remote(block, block, fs.at[c, k], fr.at[c, k], sibling)
+        block = rows.at[c, core, chip]
+        return remote(block, block, gs.at[c], gr.at[c], target(k) * 2 + core)
+
+    def across_all(c):
+        block = rows.at[c, core, pl.ds(0, chips - 1)]
+        return remote(block, block, gs.at[c], gr.at[c], sibling)
+
+    def forward(c):
+        block = rows.at[c, core]
+        return remote(block, block, fs.at[c], fr.at[c], sibling)
+
+    def backward(c):
+        block = rows.at[c, 1 - core]
+        return remote(block, block, fs.at[c], fr.at[c], sibling)
 
     for c in range(chunks):
         each(1, chips, lambda k: across(c, k).start())
-        first(c).start()
 
     def relay(c):
-        def step(k):
-            block = rows.at[c, source(k) * 2 + core]
-            remote(own.at[c], block, gs.at[c, k], gr.at[c, k], sibling).wait_recv()
-            forward(c, k).start()
-
-        each(1, chips, step)
+        across_all(c).wait_recv()
+        forward(c).start()
 
     def gathered(c):
-        def step(k):
-            block = rows.at[c, source(k) * 2 + 1 - core]
-            remote(own.at[c], block, fs.at[c, k], fr.at[c, k], sibling).wait_recv()
-
-        each(0, chips, step)
+        backward(c).wait_recv()
 
     def project(c):
         return jnp.dot(
@@ -454,20 +446,14 @@
     def start_all(src, dst, send, recv):
         def copy(k):
             peer = lax.rem(me + k, n)
-            block = src.at[peer] if len(src.shape) == len(dst.shape) else src
-            return remote(block, dst.at[me], send.at[k], recv.at[k], peer)
+            spot = lax.rem(peer, 2) * chips + peer // 2
+            block = src.at[spot] if len(src.shape) == len(dst.shape) else src
+            return remote(block, dst.at[place], send, recv, peer)
 
         each(1, n, lambda k: copy(k).start())
-
-        def arrive():
-            def take(k):
-                peer = lax.rem(me - k + n, n)
-                block = src.at[peer] if len(src.shape) == len(dst.shape) else src
-                remote(block, dst.at[peer], send.at[k], recv.at[k], peer).wait_recv()
-
-            each(1, n, take)
-
-        return arrive, lambda: each(1, n, lambda k: copy(k).wait_send())
+        many = dst.at[pl.ds(0, n - 1)]
+        every = remote(many, many, send, recv, sibling)
+        return every.wait_recv, every.wait_send
 
     relay(0)
     queries = jnp.zeros((n * height, columns), jnp.float32)
@@ -481,20 +467,20 @@
             loads[1].wait()
             share = n // chunks
             start = pl.multiple_of(lax.rem(me, share) * depth, 128)
-            piece = rows[me // share, :, :, pl.ds(start, depth)].reshape(n * height, depth)
+            piece = rows[me // share, :, :, :, pl.ds(start, depth)].reshape(n * height, depth)
             partial = jnp.dot(piece, wkv[...], preferred_element_type=jnp.float32)
             kv_from[...] = partial.reshape(n, height, 2 * HEAD_DIM)
-            kv_to[me] = kv_from[me]
-            kv_arrive, kv_sent = start_all(kv_from, kv_to, ks, kr)
+            kv_to[place] = kv_from[place]
+            kv_arrive, kv_sent = start_all(kv_from, kv_to, ks.at[0], kr.at[0])
         queries = queries + project(c)
     q_from[...] = queries.reshape(n, height * local_heads, HEAD_DIM).astype(jnp.bfloat16)
-    q_to[me] = q_from[me]
-    q_arrive, q_sent = start_all(q_from, q_to, qs, qr)
+    q_to[place] = q_from[place]
+    q_arrive, q_sent = start_all(q_from, q_to, qs.at[0], qr.at[0])
     kv_arrive()
     fresh = jnp.sum(kv_to[...], axis=0).astype(jnp.bfloat16)
     kv_own[...] = fresh
-    new_ref[me] = fresh
-    new_arrive, new_sent = start_all(kv_own, new_ref, bs, br)
+    new_ref[place] = fresh
+    new_arrive, new_sent = start_all(kv_own, new_ref, bs.at[0], br.at[0])
     q_arrive()
 
     block_rows = height * local_heads
@@ -518,7 +504,8 @@
     new_arrive()
     keyvals = new_ref[...].reshape(n * height, 2 * HEAD_DIM)
     column = lax.broadcasted_iota(jnp.int32, (count, n * height), 1)
-    owner = column // height
+    spot = column // height
+    owner = lax.rem(spot, chips) * 2 + spot // chips
     kind = lax.rem(column, height)
     reach = jnp.where(token < steps, jnp.where(chosen, n, -1), me)
     from_prefill = (kind == steps) & (owner <= reach)
@@ -535,8 +522,8 @@
         new.astype(jnp.bfloat16), keyvals[:, HEAD_DIM:], preferred_element_type=jnp.float32
     )
     mix_from[...] = (mixed / total).reshape(n, block_rows, HEAD_DIM).astype(jnp.bfloat16)
-    mix_to[me] = mix_from[me]
-    mix_arrive, mix_sent = start_all(mix_from, mix_to, ms, mr)
+    mix_to[place] = mix_from[place]
+    mix_arrive, mix_sent = start_all(mix_from, mix_to, ms.at[0], mr.at[0])
     loads[3].wait()
     mix_arrive()
     flat = mix_to[...].astype(jnp.float32).reshape(n * height, columns).astype(jnp.bfloat16)
@@ -546,9 +533,11 @@
 
     def out_across(e, k):
         to = target(k)
-        return remote(
-            pair.at[e, to], far.at[e, chip], ss.at[e, k], sr.at[e, k], to * 2 + core
-        )
+        return remote(pair.at[e, to], far.at[e, chip], ss.at[e], sr.at[e], to * 2 + core)
+
+    def out_all(e):
+        block = far.at[e, pl.ds(0, chips - 1)]
+        return remote(block, block, ss.at[e], sr.at[e], sibling)
 
     def fold(e):
         swap(e).wait_recv()
@@ -561,30 +550,21 @@
         product = jnp.dot(
             flat, wo[:, e * wide : (e + 1) * wide], preferred_element_type=jnp.float32
         )
-        product = product.reshape(chips, 2, height, wide).astype(jnp.bfloat16)
-        part[e, 0] = product[:, 0]
-        part[e, 1] = product[:, 1]
+        part[e] = product.reshape(2, chips, height, wide).astype(jnp.bfloat16)
         swap(e).start()
         if e > 0:
             fold(e - 1)
     fold(chunks - 1)
     for e in range(chunks):
-
-        def take(k):
-            remote(
-                pair.at[e, 0], far.at[e, source(k)], ss.at[e, k], sr.at[e, k], sibling
-            ).wait_recv()
-
-        each(1, chips, take)
+        out_all(e).wait_recv()
         result = jnp.sum(far[e].astype(jnp.float32), axis=0).astype(jnp.bfloat16)
         dec_out[:, e * wide : (e + 1) * wide] = result[:steps]
         pre_out[:, e * wide : (e + 1) * wide] = result[steps:]
     for c in range(chunks):
-        each(1, chips, lambda k: across(c, k).wait_send())
-        first(c).wait_send()
-        each(1, chips, lambda k: forward(c, k).wait_send())
+        across_all(c).wait_send()
+        forward(c).wait_send()
         swap(c).wait_send()
-        each(1, chips, lambda k: out_across(c, k).wait_send())
+        out_all(c).wait_send()
     kv_sent()
     q_sent()
     new_sent()
@@ -597,7 +577,7 @@
     height = steps + 1
     columns = wq.shape[1]
     local_heads = columns // HEAD_DIM
-    chunks = 4
+    chunks = 2
     wide = width // chunks
     chips = n // 2
     heads_block = (n, height * local_heads, HEAD_DIM)
@@ -618,8 +598,7 @@
             pltpu.VMEM(wq.shape, narrow),
             pltpu.VMEM(wkv.shape, narrow),
             pltpu.VMEM(wo.shape, narrow),
-            pltpu.VMEM((chunks, height, wide), narrow),
-            pltpu.VMEM((chunks, n, height, wide), narrow),
+            pltpu.VMEM((chunks, 2, chips, height, wide), narrow),
             pltpu.VMEM(heads_block, narrow),
             pltpu.VMEM(heads_block, narrow),
             pltpu.VMEM(new_block, jnp.float32),
@@ -634,12 +613,11 @@
             pltpu.VMEM(half, narrow),
             dma((4,)),
         ]
-        + [dma((chunks, chips))] * 4
-        + [dma((n,))] * 8
-        + [dma((chunks,))] * 2
-        + [dma((chunks, chips))] * 2,
+        + [dma((chunks,))] * 4
+        + [dma((1,))] * 8
+        + [dma((chunks,))] * 4,
         compiler_params=pltpu.CompilerParams(
-            collective_id=4, has_side_effects=True, vmem_limit_bytes=48 * 1024 * 1024
+            collective_id=4, has_side_effects=True, vmem_limit_bytes=60 * 1024 * 1024
         ),
     )(length, slot, prefill, decode, gain, cache, wq, wkv, wo)
 

time: 56.6 us -> 48.8 us (0.86)
  local copies, waits for them, and re-layouts: 7.98 us -> 2.81 us
  Pallas kernels: 46.3 us -> 43.8 us
    unnamed x14 -> x2, local copies, waits for them, and re-layouts: 7.98 us -> 2.81 us
    pallas_call x1, Pallas kernels: 46.3 us -> 43.8 us  [fused(): pl.pallas_call(functools.partial(fused_kernel, n, steps, local_heads), ou...]
where the time goes in v3:
time: 48.8 us; the launch traced here: 48.5 us
  Pallas kernels  43.8 us (90%)
  local copies, waits for them, and re-layouts  2.81 us (6%)
  between operations  1.93 us (4%)
    pallas_call x1, Pallas kernels, fused(): pl.pallas_call(functools.partial(fused_kernel, n, steps, local_heads), ou...  43.8 us
    unnamed x2, local copies, waits for them, and re-layouts  2.81 us

profile of v3, /device:TPU:0, one launch (start us, length us, event | category | flops | bytes accessed | tf_op | source)
XLA Modules:
  0.0 48.5 jit_solution(16110617910013778035)
XLA Ops:
  1.9 43.8 %shard_map.104 = (bf16[1,6144]{1,0:T(2,128)(2,1)}, bf16[3,6144]{1,0:T(4,128)(2,1)}) custom-call(s32[1]{0:T(128)S(6)} %copy.13.length_ref, s32[1]{0:T(128)S(6)} %copy.14.slot_ref, bf16[1,6144]{1,0:T(2,128)(2,1)} %prefill_ref.1, bf16[3,6144]{1,0:T(4,128)(2,1)} %bitcast.5, f32[1,6144]{1,0:T(1,128)} %bitcast.7, bf16[2048,256]{1,0:T(8,128)(2,1)} %bitcast.4, ...), custom_call_target="tpu_custom_call" | custom-call | tf_op jit(solution)/shard_map/pallas_call | solution.py:588
  45.7 1.4 %copy.15 = bf16[1,6144]{1,0:T(2,128)(2,1)} copy(bf16[1,6144]{1,0:T(2,128)(2,1)} %get-tuple-element.8) | data formatting | bytes 24576
  47.1 1.4 %copy.16 = bf16[1,3,6144]{2,1,0:T(4,128)(2,1)} copy(bf16[1,3,6144]{2,1,0:T(4,128)(2,1)} %bitcast.6) | data formatting | bytes 73728
